TPU v7x, 32 devices: a whole 2x2x4 slice. The times are simulated.
32 devices in a mesh: groups: 2 (over x), gx: 16 (over z, y, core).
Axes of the slice: x: 2, y: 2, z: 4, core: 2. Of those that a mesh axis runs over, the one named last changes fastest.
Arguments:
- cotangent: float32 [4, 8, 8, 8, 16384], P(None, None, None, None, ('groups', 'gx')), parts along dimension 4, may hold values from -6 to 6
- base_velocity: float32 [3, 8, 8, 8, 16384], P(None, None, None, None, ('groups', 'gx')), parts along dimension 4, may hold values from -12 to 12
- viscosity: float32 [8, 8, 8, 16384], P(None, None, None, ('groups', 'gx')), parts along dimension 3, may hold values from 0.1 to 3, as said below
- elem_slot: int32 [32, 512], P(('groups', 'gx')), parts along dimension 0, may hold values from 0 to 511, each once within a row
Outputs:
- adjoint: float32 [4, 8, 8, 8, 16384], P(None, None, None, None, ('groups', 'gx')), parts along dimension 4
- dissipation: float32 [2], P('groups'), parts along dimension 0
There are 2 independent parts, one for each index of `groups`. A program takes and returns all parts, laid end to end along the dimension named above; each array names one. Nothing has to cross between parts.
Inputs may be any that keep to these rules, and one draw needn't show every extreme that they name: viscosity is positive.
All inputs are finite; a program needn't handle non-finite values.
Results may differ from a plain program's by a relative error of at most 0.0001.
Values sent between devices are 32-bit elements; how exact they have to be, the bound alone decides.
A program may use at most 448 MiB of HBM per device.

v0:
```python
import jax
import jax.numpy as jnp
from jax import lax
from jax.sharding import PartitionSpec as P

PY = 4
PZ = 2
EX = 8
EY = 8
EZ = 8


GLL_NODES = (
    -1.0,
    -0.8717401485096066,
    -0.5917001814331423,
    -0.2092992179024789,
    0.2092992179024789,
    0.5917001814331423,
    0.8717401485096066,
    1.0,
)


def shifted(value, axis, steps):
    count = lax.axis_size(axis)
    first, last = (max(0, -steps), min(count, count - steps))
    return lax.ppermute(value, axis, [(source, source + steps) for source in range(first, last)])


def gll_tables():
    degree = 7
    points = list(GLL_NODES)
    previous = [1.0] * 8
    current = list(points)
    for order_idx in range(1, degree):
        following = [
            ((2 * order_idx + 1) * point * now - order_idx * before) / (order_idx + 1)
            for point, now, before in zip(points, current, previous)
        ]
        previous = current
        current = following
    weights = [2.0 / (degree * (degree + 1) * value * value) for value in current]
    derivative = [[0.0] * 8 for row_idx in range(8)]
    for upper_idx in range(8):
        for lower_idx in range(8):
            if upper_idx != lower_idx:
                derivative[upper_idx][lower_idx] = current[upper_idx] / (
                    current[lower_idx] * (points[upper_idx] - points[lower_idx])
                )
    derivative[0][0] = -degree * (degree + 1) / 4.0
    derivative[7][7] = degree * (degree + 1) / 4.0
    mass_diag = [
        [
            [[weights[first] * weights[second] * weights[third]] for third in range(8)]
            for second in range(8)
        ]
        for first in range(8)
    ]
    return (jnp.asarray(derivative, jnp.float32), jnp.asarray(mass_diag, jnp.float32))


def along(derivative, values_in, direction, transpose):
    matrix = derivative.T if transpose else derivative
    forms = ("ai,ijkn->ajkn", "bj,ijkn->ibkn", "ck,ijkn->ijcn")
    return jnp.einsum(forms[direction], matrix, values_in, precision=lax.Precision.HIGHEST)


def prepare(derivative, mass_diag, cotangent, base_velocity, viscosity):
    weighted = mass_diag * viscosity
    pressure_w = mass_diag * cotangent[3]
    fluxes = []
    divergence = jnp.zeros_like(viscosity)
    dissipation = jnp.float32(0.0)
    for component in range(3):
        scaled_cot = mass_diag * cotangent[component]
        row_list = []
        for direction in range(3):
            grad_val = along(derivative, cotangent[component], direction, False)
            dissipation = dissipation + jnp.sum(weighted * grad_val * grad_val)
            flux_term = weighted * grad_val + base_velocity[direction] * scaled_cot
            if direction == component:
                flux_term = flux_term - pressure_w
                divergence = divergence + grad_val
            row_list.append(flux_term)
        fluxes.append(row_list)
    pressure_adj = -mass_diag * divergence
    return (fluxes, pressure_adj, dissipation)


def planes(derivative, fluxes, pressure_adj):
    outputs = []
    for component in range(3):
        x_part = along(derivative, fluxes[component][0], 0, True)
        y_part = along(derivative, fluxes[component][1], 1, True)
        z_part = along(derivative, fluxes[component][2], 2, True)
        outputs.append(x_part + y_part + z_part)
    outputs.append(pressure_adj)
    return jnp.stack(outputs)


def pair_local(block, direction):
    node_axis = 1 + direction
    elem_axis = 4 + direction
    count = block.shape[elem_axis]
    lower_face = lax.slice_in_dim(block, 0, 1, axis=node_axis)
    upper_face = lax.slice_in_dim(block, 7, 8, axis=node_axis)
    middle = lax.slice_in_dim(block, 1, 7, axis=node_axis)
    lower_next = lax.slice_in_dim(lower_face, 1, count, axis=elem_axis)
    upper_prev = lax.slice_in_dim(upper_face, 0, count - 1, axis=elem_axis)
    new_upper = jnp.concatenate(
        [upper_prev + lower_next, lax.slice_in_dim(upper_face, count - 1, count, axis=elem_axis)],
        elem_axis,
    )
    new_lower = jnp.concatenate(
        [lax.slice_in_dim(lower_face, 0, 1, axis=elem_axis), lower_next + upper_prev], elem_axis
    )
    return jnp.concatenate([new_lower, middle, new_upper], node_axis)


def side_index(block_shape, sides):
    index_list = [slice(None)] * 7
    for direction in range(3):
        side = sides[direction]
        if side != 0:
            count = block_shape[4 + direction]
            index_list[1 + direction] = slice(7, 8) if side > 0 else slice(0, 1)
            index_list[4 + direction] = slice(count - 1, count) if side > 0 else slice(0, 1)
    return tuple(index_list)


def shards(cotangent, base_velocity, viscosity, elem_slot):
    derivative, mass_diag = gll_tables()
    fluxes, pressure_adj, dissipation = prepare(
        derivative, mass_diag, cotangent, base_velocity, viscosity
    )
    slots = elem_slot[0]
    total = lax.psum(dissipation, "gx")
    grid = planes(derivative, fluxes, pressure_adj)[..., slots]
    block = grid.reshape((4, 8, 8, 8, EX, EY, EZ))
    blocks_x = lax.axis_size("gx") // (PY * PZ)
    strides = (PY * PZ, PZ, 1)
    counts = (blocks_x, PY, PZ)
    here = lax.axis_index("gx")
    coords = [here // strides[direction] % counts[direction] for direction in range(3)]
    for direction in range(3):
        upper_sides = [0, 0, 0]
        upper_sides[direction] = 1
        lower_sides = [0, 0, 0]
        lower_sides[direction] = -1
        upper_at = side_index(block.shape, tuple(upper_sides))
        lower_at = side_index(block.shape, tuple(lower_sides))
        from_below = shifted(block[upper_at], "gx", strides[direction])
        from_above = shifted(block[lower_at], "gx", -strides[direction])
        below_ok = (coords[direction] > 0).astype(jnp.float32)
        above_ok = (coords[direction] < counts[direction] - 1).astype(jnp.float32)
        block = pair_local(block, direction)
        block = block.at[lower_at].add(from_below * below_ok)
        block = block.at[upper_at].add(from_above * above_ok)
    grid = block.reshape(grid.shape)
    assembled = jnp.zeros_like(grid).at[..., slots].set(grid)
    average = total / jnp.float32(512.0 * slots.shape[0] * lax.axis_size("gx"))
    return (assembled, jnp.reshape(average, (1,)))


def solution(mesh):
    in_specs = (
        P(None, None, None, None, ("groups", "gx")),
        P(None, None, None, None, ("groups", "gx")),
        P(None, None, None, ("groups", "gx")),
        P(("groups", "gx"), None),
    )
    out_specs = (P(None, None, None, None, ("groups", "gx")), P("groups"))
    return jax.shard_map(shards, mesh=mesh, in_specs=in_specs, out_specs=out_specs, check_vma=False)
```

profile of v0, /device:TPU:0, one launch (start us, length us, event | category | flops | bytes accessed | tf_op | source)
XLA Modules:
  0.0 1261.4 jit_solution(11180012797793386864)
XLA Ops:
  0.7 2.3 fusion.59
  3.0 2.2 fusion.61
  5.2 2.2 fusion.57
  8.7 4.5 slice_bitcast_fusion.2
  13.2 2.2 fusion.11
  15.4 2.2 fusion.44
  17.6 2.2 fusion.42
  19.8 2.2 fusion.46
  21.9 2.2 fusion.9
  24.1 2.6 fusion.7
  26.8 13.1 %fusion.16 = (f32[]{:T(128)}, f32[]{:T(128)}, f32[]{:T(128)}, f32[]{:T(128)}, f32[]{:T(128)}, /*index=5*/f32[]{:T(128)}, f32[]{:T(128)}, f32[]{:T(128)}, f32[]{:...) fusion(f32[8,8,8,512]{3,0,2,1:T(8,128)S(1)} %fusion.57, ...), kind=kLoop, calls=%fused_computation.40 | loop fusion | flops 12845047 | bytes 24121380 | tf_op jit(solution)/shard_map/reduce_sum | solution.py:80
  39.9 2.6 fusion.32
  42.4 2.6 fusion.30
  45.0 2.6 fusion.28
  47.6 1.9 fusion.26
  49.5 1.9 fusion.22
  51.4 1.9 fusion.24
  53.3 4.9 fusion.5
  58.2 3.8 fusion.3
  62.0 4.2 fusion.1
  66.2 2.5 pad_maximum_fusion
  68.7 27.1 %copy.414 = f32[4,8,8,8,512]{3,2,4,1,0:T(8,128)} copy(f32[4,8,8,8,512]{4,1,3,2,0:T(8,128)} %pad_maximum_fusion) | data formatting | bytes 8388608 | tf_op jit(solution)/shard_map/stack | solution.py:99
  95.7 46.7 %gather_fusion = f32[512,4,8,8,8]{4,3,2,1,0:T(8,128)} fusion(f32[4,8,8,8,512]{3,2,4,1,0:T(8,128)} %copy.414, s32[1024]{0:T(1024)S(1)} %pad_clamp_fusion), kind=kCustom, calls=%fused_computation | custom fusion | bytes 8390656 | tf_op jit(solution)/shard_map/gather | solution.py:139
  142.4 1.8 fusion.67
  145.2 7.0 collective-permute-start
  154.3 14.0 %fusion.68 = (f32[4,1,8,8,7,8,8]{3,2,1,0,6,5,4:T(8,128)}, f32[4,1,8,8,7,8,8]{3,2,1,0,6,5,4:T(8,128)}) fusion(f32[4,8,8,8,8,8,8]{3,2,1,0,6,5,4:T(8,128)} %bitcast.38), kind=kLoop, calls=%fused_computation.119 | loop fusion | bytes 1835008 | tf_op jit(solution)/shard_map/slice | solution.py:110
  168.3 35.5 %slice.420 = f32[4,6,8,8,8,8,8]{3,2,1,0,6,5,4:T(8,128)} slice(f32[4,8,8,8,8,8,8]{3,2,1,0,6,5,4:T(8,128)} %bitcast.38), slice={[0:4], [1:7], [0:8], [0:8], [0:8], [0:8], [0:8]} | slice | bytes 6291456 | tf_op jit(solution)/shard_map/slice | solution.py:108
  203.8 52.3 %copy.465 = f32[4,6,8,8,8,8,8]{5,4,6,3,2,1,0:T(8,128)} copy(f32[4,6,8,8,8,8,8]{3,2,1,0,6,5,4:T(8,128)} %slice.420) | data formatting | bytes 6291456
  256.1 9.2 copy.464
  265.3 9.2 copy.463
  280.1 12.0 add.173
  292.2 44.1 %maximum_maximum_fusion = f32[4,8,8,8,8,8,8]{5,4,6,3,2,1,0:T(8,128)} fusion(f32[4,1,8,8,1,8,8]{5,4,6,3,2,1,0:T(1,128)S(1)} %copy.466, f32[4,1,8,8,7,8,8]{5,4,6,3,2,1,0:T(8,128)} %add.173, f32[4,6,8,8,8,8,8]{5,4,6,3,2,1,0:T(8,128)} %copy.465, f32[4,1,8,8,1,8,8]{5,4,6,3,2,1,0:T(1,128)S(1)} %copy.462), kind=kLoop, calls=%fused_computation.2 | loop fusion | flops 4194304 | bytes 7929856 | tf_op jit(solution)/shard_map/concatenate | solution.py:118
  336.3 34.6 %psum.7 = f32[]{:T(128)} all-reduce(f32[]{:T(128)S(6)} %add.192), channel_id=1, replica_groups=mesh['groups'=2,'gx'=16] {'gx'}, use_global_device_ids=true, to_apply=%region_10.11 | all-reduce | flops 1 | bytes 8 | tf_op jit(solution)/shard_map/psum | solution.py:138
  371.5 1.4 multiply_add_fusion
  372.9 27.9 %scatter-add.20 = f32[4,8,8,8,8,8,8]{5,4,6,3,2,1,0:T(8,128)} dynamic-update-slice(f32[4,8,8,8,8,8,8]{5,4,6,3,2,1,0:T(8,128)} %maximum_maximum_fusion, f32[4,1,8,8,1,8,8]{5,4,6,3,2,1,0:T(1,128)S(1)} %bitcast.217, s32[]{:T(128)} %constant.228.clone.1, s32[]{:T(128)} %constant.228.clone.1, s32[]{:T(128)} %constant.228.clone.1, s32[]{:T(128)} %constant.228.clone.1, s32[]{:T(128)} %constant.228.clone.1, ...) | dynamic-update-slice | bytes 131076 | tf_op jit(solution)/shard_map/scatter-add | solution.py:158
  400.8 5.2 slice_add_fusion.4
  406.0 27.9 %scatter-add.21 = f32[4,8,8,8,8,8,8]{5,4,6,3,2,1,0:T(8,128)} dynamic-update-slice(f32[4,8,8,8,8,8,8]{5,4,6,3,2,1,0:T(8,128)} %scatter-add.20, f32[4,1,8,8,1,8,8]{5,4,6,3,2,1,0:T(1,128)S(1)} %slice_add_fusion.4, s32[]{:T(128)} %constant.228.clone.1, s32[]{:T(128)} %constant.232.clone.1, s32[]{:T(128)} %constant.228.clone.1, s32[]{:T(128)} %constant.228.clone.1, s32[]{:T(128)} %constant.232.clone.1, ...) | dynamic-update-slice | bytes 131076 | tf_op jit(solution)/shard_map/scatter-add | solution.py:159
  433.9 8.9 slice.427
  442.8 13.8 %copy.421 = f32[4,8,1,8,8,1,8]{6,4,5,3,2,1,0:T(8,128)S(1)} copy(f32[4,8,1,8,8,1,8]{5,4,6,3,2,1,0:T(8,128)} %slice.427) | data formatting | bytes 131072 | tf_op jit(solution)/shard_map/slice | solution.py:112
  456.6 1.6 collective-permute-start.2
  458.1 12.0 slice_add_fusion.1
  470.1 35.0 %slice.426 = f32[4,8,6,8,8,8,8]{5,4,6,3,2,1,0:T(8,128)} slice(f32[4,8,8,8,8,8,8]{5,4,6,3,2,1,0:T(8,128)} %scatter-add.21), slice={[0:4], [0:8], [1:7], [0:8], [0:8], [0:8], [0:8]} | slice | bytes 6291456 | tf_op jit(solution)/shard_map/slice | solution.py:108
  505.2 13.6 %copy.423 = f32[4,8,1,8,8,1,8]{5,4,6,3,2,1,0:T(8,128)} copy(f32[4,8,1,8,8,1,8]{6,4,5,3,2,1,0:T(8,128)S(1)} %broadcast_multiply_fusion.1) | data formatting | bytes 131072 | tf_op jit(solution)/shard_map/mul | solution.py:158
  518.7 11.0 slice_add_fusion.5
  529.8 13.8 %copy.424 = f32[4,8,1,8,8,1,8]{6,4,5,3,2,1,0:T(8,128)S(1)} copy(f32[4,8,1,8,8,1,8]{5,4,6,3,2,1,0:T(8,128)} %get-tuple-element.102) | data formatting | bytes 131072 | tf_op jit(solution)/shard_map/slice | solution.py:116
  543.5 1.5 collective-permute-start.3
  545.1 50.2 %maximum_maximum_fusion.1 = f32[4,8,8,8,8,8,8]{5,4,6,3,2,1,0:T(8,128)} fusion(f32[4,8,1,8,8,1,8]{5,4,6,3,2,1,0:T(8,128)} %slice.427, f32[4,8,1,8,8,7,8]{5,4,6,3,2,1,0:T(8,128)} %slice_add_fusion.1, f32[4,8,6,8,8,8,8]{5,4,6,3,2,1,0:T(8,128)} %slice.426, f32[4,8,1,8,8,1,8]{5,4,6,3,2,1,0:T(8,128)} %get-tuple-element.102), kind=kLoop, calls=%fused_computation.3 | loop fusion | flops 4194304 | bytes 7929856 | tf_op jit(solution)/shard_map/concatenate | solution.py:118
  595.3 28.1 %scatter-add.24 = f32[4,8,8,8,8,8,8]{5,4,6,3,2,1,0:T(8,128)} dynamic-update-slice(f32[4,8,8,8,8,8,8]{5,4,6,3,2,1,0:T(8,128)} %maximum_maximum_fusion.1, f32[4,8,1,8,8,1,8]{5,4,6,3,2,1,0:T(8,128)} %get-tuple-element.101, s32[]{:T(128)} %constant.228.clone.1, s32[]{:T(128)} %constant.228.clone.1, s32[]{:T(128)} %constant.228.clone.1, s32[]{:T(128)} %constant.228.clone.1, s32[]{:T(128)} %constant.228.clone.1, ...) | dynamic-update-slice | bytes 131076 | tf_op jit(solution)/shard_map/scatter-add | solution.py:158
  623.4 13.5 %copy.426 = f32[4,8,1,8,8,1,8]{5,4,6,3,2,1,0:T(8,128)} copy(f32[4,8,1,8,8,1,8]{6,4,5,3,2,1,0:T(8,128)S(1)} %broadcast_multiply_fusion) | data formatting | bytes 131072 | tf_op jit(solution)/shard_map/mul | solution.py:159
  637.0 11.9 slice_add_fusion
  648.9 163.9 %scatter-add.25 = f32[4,8,8,8,8,8,8]{5,4,6,3,2,1,0:T(8,128)} dynamic-update-slice(f32[4,8,8,8,8,8,8]{5,4,6,3,2,1,0:T(8,128)} %scatter-add.24, f32[4,8,1,8,8,1,8]{5,4,6,3,2,1,0:T(8,128)} %slice_add_fusion, s32[]{:T(128)} %constant.228.clone.1, s32[]{:T(128)} %constant.228.clone.1, s32[]{:T(128)} %constant.232.clone.1, s32[]{:T(128)} %constant.228.clone.1, s32[]{:T(128)} %constant.228.clone.1, ...) | dynamic-update-slice | bytes 131076 | tf_op jit(solution)/shard_map/scatter-add | solution.py:159
  812.8 1.7 fusion.66
  814.5 9.5 slice_add_fusion.2
  823.9 35.0 %slice.432 = f32[4,8,8,6,8,8,8]{5,4,6,3,2,1,0:T(8,128)} slice(f32[4,8,8,8,8,8,8]{5,4,6,3,2,1,0:T(8,128)} %scatter-add.25), slice={[0:4], [0:8], [0:8], [1:7], [0:8], [0:8], [0:8]} | slice | bytes 6291456 | tf_op jit(solution)/shard_map/slice | solution.py:108
  860.2 3.4 collective-permute-start.4
  863.6 44.6 %maximum_maximum_fusion.2 = f32[4,8,8,8,8,8,8]{5,4,6,3,2,1,0:T(8,128)} fusion(f32[4,8,8,1,8,8,1]{5,4,6,3,2,1,0:T(8,128)S(1)} %get-tuple-element.100, f32[4,8,8,1,8,8,7]{5,4,6,3,2,1,0:T(8,128)} %slice_add_fusion.2, f32[4,8,8,6,8,8,8]{5,4,6,3,2,1,0:T(8,128)} %slice.432, f32[4,8,8,1,8,8,1]{5,4,6,3,2,1,0:T(8,128)S(1)} %get-tuple-element.99), kind=kLoop, calls=%fused_computation.4 | loop fusion | flops 4194304 | bytes 7929856 | tf_op jit(solution)/shard_map/concatenate | solution.py:118
  908.2 2.4 add_dynamic-update-slice_fusion
  910.6 2.4 fusion.6
  913.0 63.0 %copy.427 = f32[4,8,8,8,8,8,8]{6,5,4,3,2,1,0:T(8,128)} copy(f32[4,8,8,8,8,8,8]{5,4,6,3,2,1,0:T(8,128)} %fusion.6) | data formatting | bytes 8388608 | tf_op jit(solution)/shard_map/scatter-add | solution.py:159
  976.0 48.3 %reshape.374 = f32[4,8,8,8,512]{4,3,2,1,0:T(8,128)} reshape(f32[4,8,8,8,8,8,8]{6,5,4,3,2,1,0:T(8,128)} %copy.427) | data formatting | bytes 8388608 | tf_op jit(solution)/shard_map/reshape | solution.py:160
  1024.3 50.2 %copy.428 = f32[512,4,8,8,8]{4,3,2,1,0:T(8,128)} copy(f32[512,4,8,8,8]{0,4,3,2,1:T(8,128)} %bitcast.215) | data formatting | bytes 8388608 | tf_op jit(solution)/shard_map/reshape | solution.py:160
  1074.4 21.0 %broadcast_in_dim.2 = f32[4,8,8,8,512]{3,2,4,1,0:T(8,128)} broadcast(f32[]{:T(128)} %constant.227.clone.1), dimensions={} | broadcast | bytes 4194308 | tf_op jit(solution)/shard_map/broadcast_in_dim | solution.py:161
  1095.4 125.2 %scatter_fusion = f32[4,8,8,8,512]{3,2,4,1,0:T(8,128)} fusion(f32[4,8,8,8,512]{3,2,4,1,0:T(8,128)} %broadcast_in_dim.2, s32[512]{0:T(512)S(1)} %bitcast.219, f32[512,4,8,8,8]{4,3,2,1,0:T(8,128)} %copy.428), kind=kCustom, calls=%fused_computation.1 | custom fusion | bytes 12584960 | tf_op jit(solution)/shard_map/scatter | solution.py:161
  1220.7 39.1 %copy.429 = f32[4,8,8,8,512]{4,3,2,1,0:T(8,128)} copy(f32[4,8,8,8,512]{3,2,4,1,0:T(8,128)} %scatter_fusion) | data formatting | bytes 8388608
  (24 shorter events, 6.0 us)
Async XLA Ops:
  0.6 47.0 %copy-start.1 = (f32[8,8,1,1]{1,0,3,2:T(8,128)S(1)}, f32[8,8,1,1]{1,0,3,2:T(8,128)}, u32[]{:S(2)}) copy-start(f32[8,8,1,1]{1,0,3,2:T(8,128)} %constant.244) | copy-start | bytes 772
  0.6 52.7 %copy-start.2 = (f32[8,8,8]{0,2,1:T(8,128)S(1)}, f32[8,8,8]{0,2,1:T(8,128)}, u32[]{:S(2)}) copy-start(f32[8,8,8]{0,2,1:T(8,128)} %constant.241) | copy-start | bytes 6148
  0.7 52.7 %copy-start = (f32[8,8,8,512]{3,2,1,0:T(8,128)S(1)}, f32[8,8,8,512]{3,2,1,0:T(8,128)}, u32[]{:S(2)}) copy-start(f32[8,8,8,512]{3,2,1,0:T(8,128)} %param.20) | copy-start | bytes 3145732
  8.1 0.6 copy-start.3
  145.2 226.4 %collective-permute-start = (f32[4,1,8,8,1,8,8]{5,4,6,3,2,1,0:T(1,128)S(1)}, f32[4,1,8,8,1,8,8]{5,4,6,3,2,1,0:T(1,128)}, u32[]{:S(2)}, u32[]{:S(2)}) collective-permute-start(f32[4,1,8,8,1,8,8]{5,4,6,3,2,1,0:T(1,128)S(1)} %copy.466), channel_id=1, source_target_pairs={{0,8},{1,9},{2,10},{3,11},{4,12},{5,13},{6,14},{7,15},{16,24},{17,... | collective-permute-start | bytes 196616 | tf_op jit(solution)/shard_map/ppermute | solution.py:28
  153.0 247.7 %collective-permute-start.1 = (f32[4,1,8,8,1,8,8]{5,4,6,3,2,1,0:T(1,128)S(1)}, f32[4,1,8,8,1,8,8]{5,4,6,3,2,1,0:T(1,128)S(1)}, u32[]{:S(2)}, u32[]{:S(2)}) collective-permute-start(f32[4,1,8,8,1,8,8]{5,4,6,3,2,1,0:T(1,128)S(1)} %copy.462), channel_id=1, source_target_pairs={{8,0},{9,1},{10,2},{11,3},{12,4},{13,5},{14,6},{15,7},{24,16},{25,... | collective-permute-start | bytes 196616 | tf_op jit(solution)/shard_map/ppermute | solution.py:28
  456.6 48.5 %collective-permute-start.2 = (f32[4,8,1,8,8,1,8]{6,4,5,3,2,1,0:T(8,128)S(1)}, f32[4,8,1,8,8,1,8]{6,4,5,3,2,1,0:T(8,128)S(1)}, u32[]{:S(2)}, u32[]{:S(2)}) collective-permute-start(f32[4,8,1,8,8,1,8]{6,4,5,3,2,1,0:T(8,128)S(1)} %copy.421), channel_id=1, source_target_pairs={{0,2},{1,3},{2,4},{3,5},{4,6},{5,7},{6,8},{7,9},{8,10},{9,11},{10,... | collective-permute-start | bytes 196616 | tf_op jit(solution)/shard_map/ppermute | solution.py:28
  543.5 79.8 %collective-permute-start.3 = (f32[4,8,1,8,8,1,8]{6,4,5,3,2,1,0:T(8,128)S(1)}, f32[4,8,1,8,8,1,8]{6,4,5,3,2,1,0:T(8,128)S(1)}, u32[]{:S(2)}, u32[]{:S(2)}) collective-permute-start(f32[4,8,1,8,8,1,8]{6,4,5,3,2,1,0:T(8,128)S(1)} %copy.424), channel_id=1, source_target_pairs={{2,0},{3,1},{4,2},{5,3},{6,4},{7,5},{8,6},{9,7},{10,8},{11,9},{12,... | collective-permute-start | bytes 196616 | tf_op jit(solution)/shard_map/ppermute | solution.py:28
  858.9 51.7 %collective-permute-start.5 = (f32[4,8,8,1,8,8,1]{5,4,6,3,2,1,0:T(8,128)S(1)}, f32[4,8,8,1,8,8,1]{5,4,6,3,2,1,0:T(8,128)S(1)}, u32[]{:S(2)}, u32[]{:S(2)}) collective-permute-start(f32[4,8,8,1,8,8,1]{5,4,6,3,2,1,0:T(8,128)S(1)} %get-tuple-element.99), channel_id=1, source_target_pairs={{1,0},{2,1},{3,2},{4,3},{5,4},{6,5},{7,6},{8,7},{9,8},{10,9},{11,1... | collective-permute-start | bytes 196616 | tf_op jit(solution)/shard_map/ppermute | solution.py:28
  860.2 48.0 %collective-permute-start.4 = (f32[4,8,8,1,8,8,1]{5,4,6,3,2,1,0:T(8,128)S(1)}, f32[4,8,8,1,8,8,1]{5,4,6,3,2,1,0:T(8,128)S(1)}, u32[]{:S(2)}, u32[]{:S(2)}) collective-permute-start(f32[4,8,8,1,8,8,1]{5,4,6,3,2,1,0:T(8,128)S(1)} %get-tuple-element.100), channel_id=1, source_target_pairs={{0,1},{1,2},{2,3},{3,4},{4,5},{5,6},{6,7},{7,8},{8,9},{9,10},{10,1... | collective-permute-start | bytes 196616 | tf_op jit(solution)/shard_map/ppermute | solution.py:28
  1024.3 71.2 %copy-start.4 = (s32[512,1]{0,1:T(1,128)S(1)}, s32[512,1]{0,1:T(1,128)}, u32[]{:S(2)}) copy-start(s32[512,1]{0,1:T(1,128)} %copy-done.3) | copy-start | bytes 6148
where the time goes:
time: 1280 us; the launch traced here: 1260 us
  local copies, waits for them, and re-layouts  932 us (73%)
  other arithmetic  223 us (17%)
  matrix products  46.5 us (4%)
  blocking collectives  34.6 us (3%)
  starting transfers between devices  16 us (1%)
    scatter-add x3, local copies, waits for them, and re-layouts, shards(): block = block.at[upper_at].add(from_above * above_ok)  255 us
    concatenate x3, other arithmetic, pair_local(): return jnp.concatenate([new_lower, middle, new_upper], node_axis)  139 us
    scatter x1, local copies, waits for them, and re-layouts, shards(): assembled = jnp.zeros_like(grid).at[..., slots].set(grid)  125 us
    unnamed x16, local copies, waits for them, and re-layouts  112 us
    slice x3, local copies, waits for them, and re-layouts, pair_local(): middle = lax.slice_in_dim(block, 1, 7, axis=node_axis)  105 us
    reshape x2, local copies, waits for them, and re-layouts, shards(): grid = block.reshape(grid.shape)  98.5 us
    scatter-add x2, local copies, waits for them, and re-layouts, shards(): block = block.at[lower_at].add(from_below * below_ok)  55.9 us
    gather x1, local copies, waits for them, and re-layouts, shards(): grid = planes(derivative, fluxes, pressure_adj)[..., slots]  46.7 us
  transfers between devices with their start and end apart: 6, of which 0 were waited for; matrix products, arithmetic and copies ran while one was open for 30% of the time, Pallas kernels for 0%

commit v1 on v0

v1 whole, which is shorter than its diff:
```python
import functools

import jax
import jax.numpy as jnp
import numpy as np
from jax import lax
from jax.experimental import pallas as pl
from jax.experimental.pallas import tpu as pltpu
from jax.sharding import PartitionSpec as P

PY = 4
PZ = 2
F32 = jnp.float32
BF16 = jnp.bfloat16
STRIDE = (64, 8, 1)
GROUPS = ((0, 1), (2, 3))

GLL_NODES = (
    -1.0,
    -0.8717401485096066,
    -0.5917001814331423,
    -0.2092992179024789,
    0.2092992179024789,
    0.5917001814331423,
    0.8717401485096066,
    1.0,
)


def gll_tables():
    degree = 7
    points = np.array(GLL_NODES)
    previous = np.ones(8)
    current = points.copy()
    for order_idx in range(1, degree):
        following = ((2 * order_idx + 1) * points * current - order_idx * previous) / (order_idx + 1)
        previous, current = current, following
    weights = 2.0 / (degree * (degree + 1) * current * current)
    derivative = np.zeros((8, 8))
    for a in range(8):
        for b in range(8):
            if a != b:
                derivative[a, b] = current[a] / (current[b] * (points[a] - points[b]))
    derivative[0, 0] = -degree * (degree + 1) / 4.0
    derivative[7, 7] = degree * (degree + 1) / 4.0
    return derivative, weights


DM, WEIGHTS = gll_tables()
BACK = DM.T * WEIGHTS[None, :] / WEIGHTS[:, None]


def hi_lo(matrix):
    high = np.asarray(matrix, np.float32).astype(jnp.bfloat16)
    low = (np.asarray(matrix, np.float64) - high.astype(np.float64)).astype(np.float32).astype(jnp.bfloat16)
    return high, low


def constants():
    eye = np.eye(8)
    forward = np.concatenate([np.kron(DM, eye), np.kron(eye, DM)], 0)
    high, low = hi_lo(forward)
    forward_lhs = np.concatenate([high, low, high, low], 1)
    backward = np.concatenate([np.kron(BACK, eye), np.kron(eye, BACK)], 1)
    high, low = hi_lo(backward)
    backward_lhs = np.concatenate([np.concatenate([high, high], 1), np.concatenate([low, low], 1)], 0)
    mass = (
        WEIGHTS[:, None, None, None] * WEIGHTS[None, :, None, None] * WEIGHTS[None, None, :, None]
        * np.ones((1, 1, 1, 128))
    ).astype(np.float32)
    return jnp.asarray(forward_lhs), jnp.asarray(backward_lhs), jnp.asarray(mass)


def apply_odd(table, xs):
    even = [xs[b] + xs[7 - b] for b in range(4)]
    odd = [xs[b] - xs[7 - b] for b in range(4)]
    ys = [None] * 8
    for a in range(4):
        first = None
        second = None
        for b in range(4):
            plus = float((table[a, b] + table[a, 7 - b]) / 2)
            minus = float((table[a, b] - table[a, 7 - b]) / 2)
            first = plus * even[b] if first is None else first + plus * even[b]
            second = minus * odd[b] if second is None else second + minus * odd[b]
        ys[a] = second + first
        ys[7 - a] = second - first
    return ys


def split(x):
    high = x.astype(BF16)
    low = (x - high.astype(F32)).astype(BF16)
    return high, low


def dot(a, b):
    return jnp.dot(a, b, preferred_element_type=F32)


def onehot(mask):
    return jnp.where(mask, F32(1.0), F32(0.0)).astype(BF16)


def kernel(
    n_gx, cot_hbm, vel_hbm, visc_hbm, slot_ref, fwd_ref, bwd_ref, mass_ref, out_hbm, diss_ref,
    cot, vel, visc, loc, near, pick, place, send, halo, part, total,
    in_sem, out_sem, send_sem, recv_sem, part_send, part_recv,
):
    me = lax.axis_index("gx")
    counts = (n_gx // (PY * PZ), PY, PZ)
    strides = (PY * PZ, PZ, 1)
    coords = [(me // strides[d]) % counts[d] for d in range(3)]

    def load(src, dst, at):
        copy = pltpu.make_async_copy(src, dst, in_sem.at[at])
        copy.start()
        return copy

    loads = [
        load(cot_hbm.at[0], cot.at[0], 0),
        load(visc_hbm, visc, 1),
        load(vel_hbm.at[0], vel.at[0], 2),
        load(cot_hbm.at[3], cot.at[3], 3),
        load(vel_hbm.at[1], vel.at[1], 4),
        load(vel_hbm.at[2], vel.at[2], 5),
        load(cot_hbm.at[1], cot.at[1], 6),
        load(cot_hbm.at[2], cot.at[2], 7),
    ]

    halo[...] = jnp.zeros_like(halo)
    total[...] = jnp.zeros_like(total)
    barrier = pltpu.get_barrier_semaphore()
    for off in range(1, n_gx):
        pl.semaphore_signal(
            barrier, inc=1, device_id={"gx": lax.rem(me + off, n_gx)},
            device_id_type=pl.DeviceIdType.MESH,
        )

    slots = slot_ref[...]
    where_is = onehot(lax.broadcasted_iota(jnp.int32, (512, 512), 0) == slots)
    at_row = lax.broadcasted_iota(jnp.int32, (16, 512), 1)
    at_col = lax.broadcasted_iota(jnp.int32, (512, 128), 0)

    def code_of(at, form):
        parts = []
        for piece in (at // 8, at % 8):
            value = piece.astype(F32).astype(BF16)
            parts.append(form(value))
        return 8.0 * parts[0] + parts[1]

    row = code_of(at_row, lambda v: lax.dot_general(v, where_is, (((1,), (1,)), ((), ())), preferred_element_type=F32))
    row = row[0:1].astype(jnp.int32)
    col = code_of(at_col, lambda v: dot(where_is, v)).astype(jnp.int32)[:, 0:1]
    for d in range(3):
        step = STRIDE[d]
        place_of = (row // step) % 8
        near[d, 0] = onehot(col == jnp.where(place_of < 7, row + step, -1))
        near[d, 1] = onehot(col == jnp.where(place_of > 0, row - step, -1))
        face = (row // (8 * step)) * step + row % step
        lane = lax.broadcasted_iota(jnp.int32, (1, 128), 1)
        sub = lax.broadcasted_iota(jnp.int32, (128, 512), 0)
        for side in range(2):
            edge = 7 * side
            for which in range(2):
                q = lane - 64 * which
                inside = (q >= 0) & (q < 64)
                q = jnp.where(inside, q, 0)
                code = (q // step) * (8 * step) + edge * step + q % step
                pick[d, side, which] = onehot(col == jnp.where(inside, code, -1))
                place[d, side, which] = onehot(
                    sub == jnp.where(place_of == edge, face + 64 * which, -1)
                )

    def component(c):
        if c == 0:
            for at in (0, 1, 2, 3):
                loads[at].wait()
        else:
            loads[5 + c].wait()

        @pl.loop(0, 8)
        def _(j):
            accumulated = total[...]
            for tile in range(4):
                ls = slice(128 * tile, 128 * tile + 128)
                u = [cot[c, i, j, :, ls] for i in range(8)]
                grad = apply_odd(DM, u)
                flux = []
                for i in range(8):
                    scaled = visc[i, j, :, ls] * grad[i]
                    accumulated = accumulated + mass_ref[i, j] * (scaled * grad[i])
                    term = scaled + vel[0, i, j, :, ls] * u[i]
                    if c == 0:
                        term = term - cot[3, i, j, :, ls]
                        loc[3, i, j, :, ls] = grad[i]
                    flux.append(term)
                result = apply_odd(BACK, flux)
                for i in range(8):
                    loc[c, i, j, :, ls] = result[i]
            total[...] = accumulated

        if c == 0:
            loads[4].wait()
            loads[5].wait()

        @pl.loop(0, 8)
        def _(i):
            mass = mass_ref[i].reshape(64, 128)
            mass = jnp.concatenate([mass, mass], 1)
            for half in range(2):
                ls = slice(256 * half, 256 * half + 256)

                def take(ref, *at):
                    return ref[(*at, i, slice(None), slice(None), ls)].reshape(64, 256)

                u = take(cot, c)
                high, low = split(u)
                grad = dot(fwd_ref[...], jnp.concatenate([high, high, low, low], 0))
                grads = (grad[:64], grad[64:])
                nu = take(visc)
                fluxes = []
                energy = None
                for d in (1, 2):
                    g = grads[d - 1]
                    scaled = nu * g
                    energy = scaled * g if energy is None else energy + scaled * g
                    term = scaled + take(vel, d) * u
                    if d == c:
                        term = term - take(cot, 3)
                        div = take(loc, 3) + g
                        if c == 2:
                            div = -mass * div
                        loc[3, i, :, :, ls] = div.reshape(8, 8, 256)
                    fluxes.append(term)
                energy = jnp.sum((mass * energy).reshape(8, 8, 256), 0)
                total[...] += energy[:, :128] + energy[:, 128:]
                high, low = split(jnp.concatenate(fluxes, 0))
                back = dot(bwd_ref[...], jnp.concatenate([high, low], 0))
                value = mass * (take(loc, c) + back[:64] + back[64:])
                loc[c, i, :, :, ls] = value.reshape(8, 8, 256)

    def face_at(c, d, side):
        index = [c, slice(None), slice(None), slice(None), slice(None)]
        index[1 + d] = 7 * side
        return tuple(index)

    def get_face(c, d, side):
        return loc[face_at(c, d, side)].reshape(64, 512)

    def put_face(c, d, side, value):
        loc[face_at(c, d, side)] = value.reshape(8, 8, 512)

    def exists(d, side):
        return coords[d] < counts[d] - 1 if side else coords[d] > 0

    def remote(g, d, side):
        partner = me + strides[d] if side else me - strides[d]
        return pltpu.make_async_remote_copy(
            src_ref=send.at[g, d, side],
            dst_ref=halo.at[g, d, 1 - side],
            send_sem=send_sem.at[g, d, side],
            recv_sem=recv_sem.at[g, d, 1 - side],
            device_id={"gx": partner},
            device_id_type=pl.DeviceIdType.MESH,
        )

    def start_stage(g, d):
        comps = GROUPS[g]
        faces = {}
        for side in range(2):
            message = None
            for which in range(2):
                value = get_face(comps[which], d, side)
                stacked = jnp.concatenate(split(value), 0)
                faces[side, which] = (value, stacked)
                piece = dot(stacked, pick[d, side, which])
                message = piece if message is None else message + piece
            send[g, d, side] = message[:64] + message[64:]

            @pl.when(exists(d, side))
            def _():
                remote(g, d, side).start()

        for side in range(2):
            other = jnp.concatenate([faces[1 - side, 0][1], faces[1 - side, 1][1]], 0)
            moved = dot(other, near[d, 1 - side])
            for which in range(2):
                value = faces[side, which][0]
                base = 128 * which
                value = value + (moved[base:base + 64] + moved[base + 64:base + 128])
                put_face(comps[which], d, side, value)

    def end_stage(g, d):
        comps = GROUPS[g]
        for side in range(2):
            @pl.when(exists(d, side))
            def _():
                copy = pltpu.make_async_remote_copy(
                    src_ref=send.at[g, d, side],
                    dst_ref=halo.at[g, d, side],
                    send_sem=send_sem.at[g, d, side],
                    recv_sem=recv_sem.at[g, d, side],
                    device_id={"gx": me + strides[d] if side else me - strides[d]},
                    device_id_type=pl.DeviceIdType.MESH,
                )
                copy.wait_recv()
                copy.wait_send()

            stacked = jnp.concatenate(split(halo[g, d, side]), 0)
            for which in range(2):
                moved = dot(stacked, place[d, side, which])
                c = comps[which]
                put_face(c, d, side, get_face(c, d, side) + (moved[:64] + moved[64:]))

    def store(g):
        copies = []
        for c in GROUPS[g]:
            copy = pltpu.make_async_copy(loc.at[c], out_hbm.at[c], out_sem.at[c])
            copy.start()
            copies.append(copy)
        return copies

    def part_copy(off, slot):
        return pltpu.make_async_remote_copy(
            src_ref=part.at[me],
            dst_ref=part.at[slot],
            send_sem=part_send.at[off],
            recv_sem=part_recv.at[off],
            device_id={"gx": lax.rem(me + off, n_gx)},
            device_id_type=pl.DeviceIdType.MESH,
        )

    component(0)
    component(1)
    pl.semaphore_wait(barrier, n_gx - 1)
    start_stage(0, 0)
    component(2)
    part[me] = total[...]
    for off in range(1, n_gx):
        part_copy(off, me).start()
    start_stage(1, 0)
    end_stage(0, 0)
    start_stage(0, 1)
    end_stage(1, 0)
    start_stage(1, 1)
    end_stage(0, 1)
    start_stage(0, 2)
    end_stage(1, 1)
    start_stage(1, 2)
    end_stage(0, 2)
    copies = store(0)
    for off in range(1, n_gx):
        part_copy(off, lax.rem(me + n_gx - off, n_gx)).wait_recv()
        part_copy(off, me).wait_send()
    end_stage(1, 2)
    copies += store(1)
    summed = part[0]
    for at in range(1, n_gx):
        summed = summed + part[at]
    diss_ref[0] = jnp.sum(summed) / F32(512.0 * 512.0 * n_gx)
    for copy in copies:
        copy.wait()


def shards(cotangent, base_velocity, viscosity, elem_slot):
    n_gx = lax.axis_size("gx")
    forward, backward, mass = constants()
    hbm = pl.BlockSpec(memory_space=pl.ANY)
    vmem = pl.BlockSpec(memory_space=pltpu.VMEM)
    return pl.pallas_call(
        functools.partial(kernel, n_gx),
        out_shape=(
            jax.ShapeDtypeStruct((4, 8, 8, 8, 512), F32),
            jax.ShapeDtypeStruct((1,), F32),
        ),
        in_specs=[hbm, hbm, hbm, vmem, vmem, vmem, vmem],
        out_specs=(hbm, pl.BlockSpec(memory_space=pltpu.SMEM)),
        scratch_shapes=[
            pltpu.VMEM((4, 8, 8, 8, 512), F32),
            pltpu.VMEM((3, 8, 8, 8, 512), F32),
            pltpu.VMEM((8, 8, 8, 512), F32),
            pltpu.VMEM((4, 8, 8, 8, 512), F32),
            pltpu.VMEM((3, 2, 512, 512), BF16),
            pltpu.VMEM((3, 2, 2, 512, 128), BF16),
            pltpu.VMEM((3, 2, 2, 128, 512), BF16),
            pltpu.VMEM((2, 3, 2, 64, 128), F32),
            pltpu.VMEM((2, 3, 2, 64, 128), F32),
            pltpu.VMEM((n_gx, 8, 128), F32),
            pltpu.VMEM((8, 128), F32),
            pltpu.SemaphoreType.DMA((8,)),
            pltpu.SemaphoreType.DMA((4,)),
            pltpu.SemaphoreType.DMA((2, 3, 2)),
            pltpu.SemaphoreType.DMA((2, 3, 2)),
            pltpu.SemaphoreType.DMA((n_gx,)),
            pltpu.SemaphoreType.DMA((n_gx,)),
        ],
        compiler_params=pltpu.CompilerParams(
            collective_id=0, has_side_effects=True, vmem_limit_bytes=48 * 1024 * 1024
        ),
        cost_estimate=pl.CostEstimate(flops=6 * 10**9, bytes_accessed=12 * 2**20, transcendentals=0),
    )(cotangent, base_velocity, viscosity, elem_slot, forward, backward, mass)


def solution(mesh):
    in_specs = (
        P(None, None, None, None, ("groups", "gx")),
        P(None, None, None, None, ("groups", "gx")),
        P(None, None, None, ("groups", "gx")),
        P(("groups", "gx"), None),
    )
    out_specs = (P(None, None, None, None, ("groups", "gx")), P("groups"))
    return jax.shard_map(shards, mesh=mesh, in_specs=in_specs, out_specs=out_specs, check_vma=False)
```

time: 1280 us -> 47.8 us (0.04); the launches traced: 1260 us -> 47.4 us
  local copies, waits for them, and re-layouts: 932 us -> 11.3 us
  other arithmetic: 223 us -> 0 us
  matrix products: 46.5 us -> 0 us
  blocking collectives: 34.6 us -> 0 us
  Pallas kernels: 0 us -> 33.7 us
  starting transfers between devices: 16 us -> 0 us
    scatter-add x5 -> x0, local copies, waits for them, and re-layouts: 311 us -> none  [the longest x3 255 us: shards(): block = block.at[upper_at].add(from_above * above_ok)]
    slice x9 -> x0, local copies, waits for them, and re-layouts: 159 us -> none  [the longest x3 105 us: pair_local(): middle = lax.slice_in_dim(block, 1, 7, axis=node_axis)]
    concatenate x3 -> x0, other arithmetic: 139 us -> none  [pair_local(): return jnp.concatenate([new_lower, middle, new_upper], node_axis)]
    scatter x1 -> x0, local copies, waits for them, and re-layouts: 125 us -> none  [shards(): assembled = jnp.zeros_like(grid).at[..., slots].set(grid)]
    unnamed x16 -> x13, local copies, waits for them, and re-layouts: 112 us -> 11.3 us
    reshape x2 -> x0, local copies, waits for them, and re-layouts: 98.5 us -> none  [shards(): grid = block.reshape(grid.shape)]
    add x7 -> x0, other arithmetic: 63 us -> none  [the longest x3 33.5 us: pair_local(): lower_next + upper_prev]
    gather x1 -> x0, local copies, waits for them, and re-layouts: 46.7 us -> none  [shards(): grid = planes(derivative, fluxes, pressure_adj)[..., slots]]
  transfers between devices with their start and end apart: 6 -> 0, of which waited for: 0 -> 0; matrix products, arithmetic and copies ran while one was open for 30% -> 0% of each run, Pallas kernels for 0% -> 0%
where the time goes in v1:
time: 47.8 us; the launch traced here: 47.4 us
  Pallas kernels  33.7 us (71%)
  local copies, waits for them, and re-layouts  11.3 us (24%)
  between operations  2.4 us (5%)
    pallas_call x1, Pallas kernels, shards(): pl.pallas_call(functools.partial(kernel, n_gx), out_shape=(jax.ShapeDtype...  33.7 us
    unnamed x13, local copies, waits for them, and re-layouts  11.3 us

profile of v1, /device:TPU:0, one launch (start us, length us, event | category | flops | bytes accessed | tf_op | source)
XLA Modules:
  0.0 47.4 jit_solution(11442059112017965517)
XLA Ops:
  0.6 0.0 copy-start
  0.6 1.9 %copy-done = f32[3,8,8,8,512]{4,3,2,1,0:T(8,128)S(1)} copy-done((f32[3,8,8,8,512]{4,3,2,1,0:T(8,128)S(1)}, f32[3,8,8,8,512]{4,3,2,1,0:T(8,128)}, u32[]{:S(2)}) %copy-start) | copy-done | bytes 3145752
  2.5 0.0 copy-start.1
  2.5 1.2 %copy-done.1 = f32[8,8,8,512]{3,2,1,0:T(8,128)S(1)} copy-done((f32[8,8,8,512]{3,2,1,0:T(8,128)S(1)}, f32[8,8,8,512]{3,2,1,0:T(8,128)}, u32[]{:S(2)}) %copy-start.1) | copy-done | bytes 1048600
  3.7 0.0 copy-start.2
  3.7 0.7 %copy-done.2 = s32[1,512]{1,0:T(1,128)S(1)} copy-done((s32[1,512]{1,0:T(1,128)S(1)}, s32[1,512]{1,0:T(1,128)}, u32[]{:S(2)}) %copy-start.2) | copy-done | bytes 2072
  4.4 0.0 copy-start.3
  4.4 0.9 %copy-done.3 = f32[8,8,8,128]{3,2,1,0:T(8,128)S(1)} copy-done((f32[8,8,8,128]{3,2,1,0:T(8,128)S(1)}, f32[8,8,8,128]{3,2,1,0:T(8,128)}, u32[]{:S(2)}) %copy-start.3) | copy-done | bytes 262168
  5.4 0.0 copy-start.4
  5.4 0.8 %copy-done.4 = bf16[128,256]{1,0:T(8,128)(2,1)S(1)} copy-done((bf16[128,256]{1,0:T(8,128)(2,1)S(1)}, bf16[128,256]{1,0:T(8,128)(2,1)}, u32[]{:S(2)}) %copy-start.4) | copy-done | bytes 65560
  6.2 0.0 copy-start.5
  6.2 0.8 %copy-done.5 = bf16[128,256]{1,0:T(8,128)(2,1)S(1)} copy-done((bf16[128,256]{1,0:T(8,128)(2,1)S(1)}, bf16[128,256]{1,0:T(8,128)(2,1)}, u32[]{:S(2)}) %copy-start.5) | copy-done | bytes 65560
  7.1 33.7 %shard_map.86 = (f32[4,8,8,8,512]{4,3,2,1,0:T(8,128)}, f32[1]{0:T(128)}) custom-call(f32[4,8,8,8,512]{4,3,2,1,0:T(8,128)} %cot_hbm.1, f32[3,8,8,8,512]{4,3,2,1,0:T(8,128)S(1)} %copy-done, f32[8,8,8,512]{3,2,1,0:T(8,128)S(1)} %copy-done.1, s32[1,512]{1,0:T(1,128)S(1)} %copy-done.2, bf16[128,256]{1,0:T(8,128)(2,1)S(1)} %copy-done.5, ...), custom_call_target="tpu_custom_call" | custom-call | flops 6000000000 | bytes 12582912 | tf_op jit(solution)/shard_map/pallas_call | solution.py:371
  40.8 4.9 %copy.11 = f32[4,8,8,8,512]{4,3,2,1,0:T(8,128)} copy(f32[4,8,8,8,512]{4,3,2,1,0:T(8,128)} %get-tuple-element.4) | data formatting | bytes 8388608
Async XLA Ops:
  0.6 1.9 %copy-start = (f32[3,8,8,8,512]{4,3,2,1,0:T(8,128)S(1)}, f32[3,8,8,8,512]{4,3,2,1,0:T(8,128)}, u32[]{:S(2)}) copy-start(f32[3,8,8,8,512]{4,3,2,1,0:T(8,128)} %vel_hbm.1) | copy-start | bytes 9437188
  2.5 1.2 %copy-start.1 = (f32[8,8,8,512]{3,2,1,0:T(8,128)S(1)}, f32[8,8,8,512]{3,2,1,0:T(8,128)}, u32[]{:S(2)}) copy-start(f32[8,8,8,512]{3,2,1,0:T(8,128)} %visc_hbm.1) | copy-start | bytes 3145732
  3.7 0.7 %copy-start.2 = (s32[1,512]{1,0:T(1,128)S(1)}, s32[1,512]{1,0:T(1,128)}, u32[]{:S(2)}) copy-start(s32[1,512]{1,0:T(1,128)} %slot_ref.1) | copy-start | bytes 6148
  4.4 0.9 %copy-start.3 = (f32[8,8,8,128]{3,2,1,0:T(8,128)S(1)}, f32[8,8,8,128]{3,2,1,0:T(8,128)}, u32[]{:S(2)}) copy-start(f32[8,8,8,128]{3,2,1,0:T(8,128)} %constant.8.clone.mass_ref) | copy-start | bytes 786436
  5.4 0.8 %copy-start.4 = (bf16[128,256]{1,0:T(8,128)(2,1)S(1)}, bf16[128,256]{1,0:T(8,128)(2,1)}, u32[]{:S(2)}) copy-start(bf16[128,256]{1,0:T(8,128)(2,1)} %constant.7.clone.bwd_ref) | copy-start | bytes 196612
  6.2 0.8 %copy-start.5 = (bf16[128,256]{1,0:T(8,128)(2,1)S(1)}, bf16[128,256]{1,0:T(8,128)(2,1)}, u32[]{:S(2)}) copy-start(bf16[128,256]{1,0:T(8,128)(2,1)} %constant.6.clone.fwd_ref) | copy-start | bytes 196612

commit v2 on v1

--- a/solution.py
+++ b/solution.py
@@ -103,8 +103,8 @@
 
 
 def kernel(
-    n_gx, cot_hbm, vel_hbm, visc_hbm, slot_ref, fwd_ref, bwd_ref, mass_ref, out_hbm, diss_ref,
-    cot, vel, visc, loc, near, pick, place, send, halo, part, total,
+    n_gx, cot_hbm, vel_hbm, visc_hbm, slot_ref, fwd_hbm, bwd_hbm, mass_hbm, out_hbm, diss_ref,
+    fwd_ref, bwd_ref, mass_ref, cot, vel, visc, loc, near, pick, place, send, halo, part, other, total,
     in_sem, out_sem, send_sem, recv_sem, part_send, part_recv,
 ):
     me = lax.axis_index("gx")
@@ -112,11 +112,21 @@
     strides = (PY * PZ, PZ, 1)
     coords = [(me // strides[d]) % counts[d] for d in range(3)]
 
+    bits = (n_gx - 1).bit_length()
+
+    def exists(d, side):
+        return coords[d] < counts[d] - 1 if side else coords[d] > 0
+
     def load(src, dst, at):
         copy = pltpu.make_async_copy(src, dst, in_sem.at[at])
         copy.start()
         return copy
 
+    tables = [
+        load(mass_hbm, mass_ref, 8),
+        load(fwd_hbm, fwd_ref, 9),
+        load(bwd_hbm, bwd_ref, 10),
+    ]
     loads = [
         load(cot_hbm.at[0], cot.at[0], 0),
         load(visc_hbm, visc, 1),
@@ -131,11 +141,23 @@
     halo[...] = jnp.zeros_like(halo)
     total[...] = jnp.zeros_like(total)
     barrier = pltpu.get_barrier_semaphore()
-    for off in range(1, n_gx):
+
+    def greet(partner):
         pl.semaphore_signal(
-            barrier, inc=1, device_id={"gx": lax.rem(me + off, n_gx)},
-            device_id_type=pl.DeviceIdType.MESH,
+            barrier, inc=1, device_id={"gx": partner}, device_id_type=pl.DeviceIdType.MESH
         )
+
+    for bit in range(bits):
+        greet(me ^ (1 << bit))
+    expected = bits
+    for d in range(3):
+        for side in range(2):
+            there = exists(d, side)
+            expected = expected + there.astype(jnp.int32)
+
+            @pl.when(there)
+            def _():
+                greet(me + strides[d] if side else me - strides[d])
 
     slots = slot_ref[...]
     where_is = onehot(lax.broadcasted_iota(jnp.int32, (512, 512), 0) == slots)
@@ -174,6 +196,7 @@
 
     def component(c):
         if c == 0:
+            tables[0].wait()
             for at in (0, 1, 2, 3):
                 loads[at].wait()
         else:
@@ -203,42 +226,57 @@
         if c == 0:
             loads[4].wait()
             loads[5].wait()
-
-        @pl.loop(0, 8)
-        def _(i):
-            mass = mass_ref[i].reshape(64, 128)
-            mass = jnp.concatenate([mass, mass], 1)
-            for half in range(2):
-                ls = slice(256 * half, 256 * half + 256)
-
-                def take(ref, *at):
-                    return ref[(*at, i, slice(None), slice(None), ls)].reshape(64, 256)
-
-                u = take(cot, c)
-                high, low = split(u)
-                grad = dot(fwd_ref[...], jnp.concatenate([high, high, low, low], 0))
-                grads = (grad[:64], grad[64:])
-                nu = take(visc)
+            tables[1].wait()
+            tables[2].wait()
+
+        @pl.loop(0, 8, step=4)
+        def _(first):
+            chains = [(first + more, slice(256 * half, 256 * half + 256)) for more in range(4) for half in range(2)]
+
+            def take(ref, chain, *at):
+                i, ls = chain
+                return ref[(*at, i, slice(None), slice(None), ls)].reshape(64, 256)
+
+            grads = []
+            for chain in chains:
+                high, low = split(take(cot, chain, c))
+                grads.append(dot(fwd_ref[...], jnp.concatenate([high, high, low, low], 0)))
+            masses = []
+            energies = []
+            divs = []
+            stacks = []
+            for chain, grad in zip(chains, grads):
+                mass = mass_ref[chain[0]].reshape(64, 128)
+                mass = jnp.concatenate([mass, mass], 1)
+                u = take(cot, chain, c)
+                nu = take(visc, chain)
                 fluxes = []
                 energy = None
                 for d in (1, 2):
-                    g = grads[d - 1]
+                    g = grad[64 * (d - 1):64 * d]
                     scaled = nu * g
                     energy = scaled * g if energy is None else energy + scaled * g
-                    term = scaled + take(vel, d) * u
+                    term = scaled + take(vel, chain, d) * u
                     if d == c:
-                        term = term - take(cot, 3)
-                        div = take(loc, 3) + g
-                        if c == 2:
-                            div = -mass * div
-                        loc[3, i, :, :, ls] = div.reshape(8, 8, 256)
+                        term = term - take(cot, chain, 3)
+                        div = take(loc, chain, 3) + g
+                        divs.append(-mass * div if c == 2 else div)
                     fluxes.append(term)
                 energy = jnp.sum((mass * energy).reshape(8, 8, 256), 0)
-                total[...] += energy[:, :128] + energy[:, 128:]
+                energies.append(energy[:, :128] + energy[:, 128:])
+                masses.append(mass)
                 high, low = split(jnp.concatenate(fluxes, 0))
-                back = dot(bwd_ref[...], jnp.concatenate([high, low], 0))
-                value = mass * (take(loc, c) + back[:64] + back[64:])
-                loc[c, i, :, :, ls] = value.reshape(8, 8, 256)
+                stacks.append(jnp.concatenate([high, low], 0))
+            backs = [dot(bwd_ref[...], stack) for stack in stacks]
+            values = [
+                mass * (take(loc, chain, c) + back[:64] + back[64:])
+                for chain, mass, back in zip(chains, masses, backs)
+            ]
+            total[...] += sum(energies[1:], energies[0])
+            for at, (i, ls) in enumerate(chains):
+                loc[c, i, :, :, ls] = values[at].reshape(8, 8, 256)
+                if divs:
+                    loc[3, i, :, :, ls] = divs[at].reshape(8, 8, 256)
 
     def face_at(c, d, side):
         index = [c, slice(None), slice(None), slice(None), slice(None)]
@@ -250,9 +288,6 @@
 
     def put_face(c, d, side, value):
         loc[face_at(c, d, side)] = value.reshape(8, 8, 512)
-
-    def exists(d, side):
-        return coords[d] < counts[d] - 1 if side else coords[d] > 0
 
     def remote(g, d, side):
         partner = me + strides[d] if side else me - strides[d]
@@ -283,8 +318,8 @@
                 remote(g, d, side).start()
 
         for side in range(2):
-            other = jnp.concatenate([faces[1 - side, 0][1], faces[1 - side, 1][1]], 0)
-            moved = dot(other, near[d, 1 - side])
+            across = jnp.concatenate([faces[1 - side, 0][1], faces[1 - side, 1][1]], 0)
+            moved = dot(across, near[d, 1 - side])
             for which in range(2):
                 value = faces[side, which][0]
                 base = 128 * which
@@ -321,62 +356,103 @@
             copies.append(copy)
         return copies
 
-    def part_copy(off, slot):
+    def part_copy(bit):
         return pltpu.make_async_remote_copy(
-            src_ref=part.at[me],
-            dst_ref=part.at[slot],
-            send_sem=part_send.at[off],
-            recv_sem=part_recv.at[off],
-            device_id={"gx": lax.rem(me + off, n_gx)},
+            src_ref=part.at[bit],
+            dst_ref=other.at[bit],
+            send_sem=part_send.at[bit],
+            recv_sem=part_recv.at[bit],
+            device_id={"gx": me ^ (1 << bit)},
             device_id_type=pl.DeviceIdType.MESH,
         )
 
+    def reduce_bit(bit):
+        part_copy(bit).wait_recv()
+        part[bit + 1] = part[bit] + other[bit]
+        if bit + 1 < bits:
+            part_copy(bit + 1).start()
+
     component(0)
     component(1)
-    pl.semaphore_wait(barrier, n_gx - 1)
+    pl.semaphore_wait(barrier, expected)
     start_stage(0, 0)
     component(2)
-    part[me] = total[...]
-    for off in range(1, n_gx):
-        part_copy(off, me).start()
+    part[0] = total[...]
+    part_copy(0).start()
     start_stage(1, 0)
     end_stage(0, 0)
+    reduce_bit(0)
     start_stage(0, 1)
     end_stage(1, 0)
     start_stage(1, 1)
+    reduce_bit(1)
     end_stage(0, 1)
     start_stage(0, 2)
     end_stage(1, 1)
+    reduce_bit(2)
     start_stage(1, 2)
     end_stage(0, 2)
     copies = store(0)
-    for off in range(1, n_gx):
-        part_copy(off, lax.rem(me + n_gx - off, n_gx)).wait_recv()
-        part_copy(off, me).wait_send()
     end_stage(1, 2)
     copies += store(1)
-    summed = part[0]
-    for at in range(1, n_gx):
-        summed = summed + part[at]
-    diss_ref[0] = jnp.sum(summed) / F32(512.0 * 512.0 * n_gx)
+    for bit in range(3, bits):
+        reduce_bit(bit)
+    diss_ref[0] = jnp.sum(part[bits]) / F32(512.0 * 512.0 * n_gx)
+    for bit in range(bits):
+        part_copy(bit).wait_send()
     for copy in copies:
         copy.wait()
 
 
+def hand_over_kernel(src, dst, held, in_sem, out_sem):
+    def incoming(at):
+        return pltpu.make_async_copy(src.at[at // 2, pl.ds(4 * (at % 2), 4)], held.at[at], in_sem.at[at])
+
+    def outgoing(at):
+        return pltpu.make_async_copy(held.at[at], dst.at[at // 2, pl.ds(4 * (at % 2), 4)], out_sem.at[at])
+
+    for at in range(8):
+        incoming(at).start()
+    for at in range(8):
+        incoming(at).wait()
+        outgoing(at).start()
+    for at in range(8):
+        outgoing(at).wait()
+
+
+def hand_over(value):
+    return pl.pallas_call(
+        hand_over_kernel,
+        out_shape=jax.ShapeDtypeStruct(value.shape, F32),
+        in_specs=[pl.BlockSpec(memory_space=pl.ANY)],
+        out_specs=pl.BlockSpec(memory_space=pl.ANY),
+        scratch_shapes=[
+            pltpu.VMEM((8, 4, 8, 8, 512), F32),
+            pltpu.SemaphoreType.DMA((8,)),
+            pltpu.SemaphoreType.DMA((8,)),
+        ],
+        compiler_params=pltpu.CompilerParams(vmem_limit_bytes=60 * 1024 * 1024),
+    )(value)
+
+
 def shards(cotangent, base_velocity, viscosity, elem_slot):
     n_gx = lax.axis_size("gx")
+    bits = (n_gx - 1).bit_length()
     forward, backward, mass = constants()
     hbm = pl.BlockSpec(memory_space=pl.ANY)
     vmem = pl.BlockSpec(memory_space=pltpu.VMEM)
-    return pl.pallas_call(
+    assembled, average = pl.pallas_call(
         functools.partial(kernel, n_gx),
         out_shape=(
             jax.ShapeDtypeStruct((4, 8, 8, 8, 512), F32),
             jax.ShapeDtypeStruct((1,), F32),
         ),
-        in_specs=[hbm, hbm, hbm, vmem, vmem, vmem, vmem],
+        in_specs=[hbm, hbm, hbm, vmem, hbm, hbm, hbm],
         out_specs=(hbm, pl.BlockSpec(memory_space=pltpu.SMEM)),
         scratch_shapes=[
+            pltpu.VMEM((128, 256), BF16),
+            pltpu.VMEM((128, 256), BF16),
+            pltpu.VMEM((8, 8, 8, 128), F32),
             pltpu.VMEM((4, 8, 8, 8, 512), F32),
             pltpu.VMEM((3, 8, 8, 8, 512), F32),
             pltpu.VMEM((8, 8, 8, 512), F32),
@@ -386,20 +462,22 @@
             pltpu.VMEM((3, 2, 2, 128, 512), BF16),
             pltpu.VMEM((2, 3, 2, 64, 128), F32),
             pltpu.VMEM((2, 3, 2, 64, 128), F32),
-            pltpu.VMEM((n_gx, 8, 128), F32),
+            pltpu.VMEM((bits + 1, 8, 128), F32),
+            pltpu.VMEM((bits, 8, 128), F32),
             pltpu.VMEM((8, 128), F32),
-            pltpu.SemaphoreType.DMA((8,)),
+            pltpu.SemaphoreType.DMA((11,)),
             pltpu.SemaphoreType.DMA((4,)),
             pltpu.SemaphoreType.DMA((2, 3, 2)),
             pltpu.SemaphoreType.DMA((2, 3, 2)),
-            pltpu.SemaphoreType.DMA((n_gx,)),
-            pltpu.SemaphoreType.DMA((n_gx,)),
+            pltpu.SemaphoreType.DMA((bits,)),
+            pltpu.SemaphoreType.DMA((bits,)),
         ],
         compiler_params=pltpu.CompilerParams(
-            collective_id=0, has_side_effects=True, vmem_limit_bytes=48 * 1024 * 1024
+            collective_id=0, has_side_effects=True, vmem_limit_bytes=60 * 1024 * 1024
         ),
         cost_estimate=pl.CostEstimate(flops=6 * 10**9, bytes_accessed=12 * 2**20, transcendentals=0),
     )(cotangent, base_velocity, viscosity, elem_slot, forward, backward, mass)
+    return hand_over(assembled), average
 
 
 def solution(mesh):

time: 47.8 us -> 34.4 us (0.72)
  local copies, waits for them, and re-layouts: 11.3 us -> 0 us
  Pallas kernels: 33.7 us -> 31.9 us
    unnamed x13 -> x0, local copies, waits for them, and re-layouts: 11.3 us -> none
    pallas_call x1, Pallas kernels: 33.7 us -> 28.3 us  [shards(): pl.pallas_call(functools.partial(kernel, n_gx), out_shape=(jax.ShapeDtype...]
    pallas_call x0 -> x1, Pallas kernels: none -> 3.58 us  [hand_over(): pl.pallas_call(hand_over_kernel, out_shape=jax.ShapeDtypeStruct(value.sha...]
where the time goes in v2:
time: 34.4 us; the launch traced here: 34.3 us
  Pallas kernels  31.9 us (93%)
  between operations  2.38 us (7%)
    pallas_call x1, Pallas kernels, shards(): pl.pallas_call(functools.partial(kernel, n_gx), out_shape=(jax.ShapeDtype...  28.3 us
    pallas_call x1, Pallas kernels, hand_over(): pl.pallas_call(hand_over_kernel, out_shape=jax.ShapeDtypeStruct(value.sha...  3.58 us

profile of v2, /device:TPU:0, one launch (start us, length us, event | category | flops | bytes accessed | tf_op | source)
XLA Modules:
  0.0 34.3 jit_solution(16549004113392758083)
XLA Ops:
  0.6 28.3 %shard_map.86 = (f32[4,8,8,8,512]{4,3,2,1,0:T(8,128)}, f32[1]{0:T(128)}) custom-call(f32[4,8,8,8,512]{4,3,2,1,0:T(8,128)} %cot_hbm.1, f32[3,8,8,8,512]{4,3,2,1,0:T(8,128)} %vel_hbm.1, f32[8,8,8,512]{3,2,1,0:T(8,128)} %visc_hbm.1, s32[1,512]{1,0:T(1,128)} %slot_ref.1, bf16[128,256]{1,0:T(8,128)(2,1)} %constant.6.clone.fwd_hbm, ...), custom_call_target="tpu_custom_call" | custom-call | flops 6000000000 | bytes 12582912 | tf_op jit(solution)/shard_map/pallas_call | solution.py:444
  28.9 3.6 %shard_map.87 = f32[4,8,8,8,512]{4,3,2,1,0:T(8,128)} custom-call(f32[4,8,8,8,512]{4,3,2,1,0:T(8,128)} %get-tuple-element.4.src), custom_call_target="tpu_custom_call" | custom-call | tf_op jit(solution)/shard_map/pallas_call | solution.py:424

commit v3 on v2

--- a/solution.py
+++ b/solution.py
@@ -229,9 +229,9 @@
             tables[1].wait()
             tables[2].wait()
 
-        @pl.loop(0, 8, step=4)
+        @pl.loop(0, 8, step=8)
         def _(first):
-            chains = [(first + more, slice(256 * half, 256 * half + 256)) for more in range(4) for half in range(2)]
+            chains = [(first + more, slice(256 * half, 256 * half + 256)) for more in range(8) for half in range(2)]
 
             def take(ref, chain, *at):
                 i, ls = chain

time: 34.4 us -> 33.8 us (0.983)
  Pallas kernels: 31.9 us -> 31.3 us
    pallas_call x1, Pallas kernels: 28.3 us -> 27.7 us  [shards(): pl.pallas_call(functools.partial(kernel, n_gx), out_shape=(jax.ShapeDtype...]
where the time goes in v3:
time: 33.8 us; the launch traced here: 33.6 us
  Pallas kernels  31.3 us (93%)
  between operations  2.38 us (7%)
    pallas_call x1, Pallas kernels, shards(): pl.pallas_call(functools.partial(kernel, n_gx), out_shape=(jax.ShapeDtype...  27.7 us
    pallas_call x1, Pallas kernels, hand_over(): pl.pallas_call(hand_over_kernel, out_shape=jax.ShapeDtypeStruct(value.sha...  3.58 us

profile of v3, /device:TPU:0, one launch (start us, length us, event | category | flops | bytes accessed | tf_op | source)
XLA Modules:
  0.0 33.6 jit_solution(3715501734923895687)
XLA Ops:
  0.6 27.7 %shard_map.86 = (f32[4,8,8,8,512]{4,3,2,1,0:T(8,128)}, f32[1]{0:T(128)}) custom-call(f32[4,8,8,8,512]{4,3,2,1,0:T(8,128)} %cot_hbm.1, f32[3,8,8,8,512]{4,3,2,1,0:T(8,128)} %vel_hbm.1, f32[8,8,8,512]{3,2,1,0:T(8,128)} %visc_hbm.1, s32[1,512]{1,0:T(1,128)} %slot_ref.1, bf16[128,256]{1,0:T(8,128)(2,1)} %constant.6.clone.fwd_hbm, ...), custom_call_target="tpu_custom_call" | custom-call | flops 6000000000 | bytes 12582912 | tf_op jit(solution)/shard_map/pallas_call | solution.py:444
  28.3 3.6 %shard_map.87 = f32[4,8,8,8,512]{4,3,2,1,0:T(8,128)} custom-call(f32[4,8,8,8,512]{4,3,2,1,0:T(8,128)} %get-tuple-element.4.src), custom_call_target="tpu_custom_call" | custom-call | tf_op jit(solution)/shard_map/pallas_call | solution.py:424
